TPU v7x, 512 devices: a whole 4x4x16 slice. The times are simulated.
512 devices in a mesh: basin: 64 (over z, x), reach: 8 (over y, core).
Axes of the slice: x: 4, y: 4, z: 16, core: 2. Of those that a mesh axis runs over, the one named last changes fastest.
Arguments:
- reach_residual: float32 [384, 24, 128], P('basin', 'reach'), may hold values from -4 to 4
- chain_inv: float32 [384, 24, 128, 128], P('basin', 'reach'), may hold values from -1 to 2
- chain_link: float32 [384, 24, 128, 128], P('basin', 'reach'), may hold values from -1 to 1
- outlet_link: float32 [384, 128, 128], P('basin'), may hold values from -0.5 to 0.5
- junction_inv: float32 [384, 128, 128], P('basin'), may hold values from -1 to 1
- junction_residual: float32 [384, 128], P('basin'), may hold values from -6 to 6
- upper_junction: int32 [384], P('basin'), may hold values from 0 to 383
- lower_junction: int32 [384], P('basin'), may hold values from 0 to 383
- cell_cotangent: float32 [384, 24, 128], P('basin', 'reach'), may hold values from -4 to 4
- junction_cotangent: float32 [384, 128], P('basin'), may hold values from -6 to 6
Outputs:
- cell_update: float32 [384, 24, 128], P('basin', 'reach')
- section_update: float32 [384, 128], P('basin')
- cell_adjoint: float32 [384, 24, 128], P('basin', 'reach')
- junction_adjoint: float32 [384, 128], P('basin')
Inputs may be any that keep to these rules, and one draw needn't show every extreme that they name: `upper_junction`: junction ids. `lower_junction`: junction ids.
All inputs are finite; a program needn't handle non-finite values.
Results may differ from a plain program's by a relative error of at most 0.00014.
Values sent between devices are 32-bit elements; how exact they have to be, the bound alone decides.
No kernel may reach another device: no remote copies, remote signals or barrier semaphores. Data moves between devices by JAX's collectives and lax.ppermute only.
A program may use at most 64 MiB of HBM per device.

v0:
```python
import jax
import jax.numpy as jnp
from jax import lax
from jax.sharding import PartitionSpec as P

SWEEPS = 4
precise = lax.Precision.HIGHEST


def entering(x, axis, combine, identity, reverse):
    length, place = (lax.axis_size(axis), lax.axis_index(axis))
    everything = jax.tree.map(lambda part: lax.all_gather(part, axis), x)
    start = jax.tree.map(
        lambda part, zero: jnp.broadcast_to(jnp.asarray(zero, part.dtype), part.shape), x, identity
    )

    def lap(k, before):
        at = length - 1 - k if reverse else k
        reached = at > place if reverse else at < place
        new = combine(before, jax.tree.map(lambda part: part[at], everything))
        return jax.tree.map(lambda a, b: jnp.where(reached, a, b), new, before)

    return lax.fori_loop(0, length, lap, start)


def from_root(block, axis, holder):
    block = jnp.where(lax.axis_index(axis) == holder, block, jnp.zeros_like(block))
    return lax.psum(block, axis)


def product(former, latter):
    return jnp.einsum("sij,sjk->sik", former, latter, precision=precise)


def applied(matrix, vector):
    return jnp.einsum("sij,sj->si", matrix, vector, precision=precise)


def applied_transposed(matrix, vector):
    return jnp.einsum("sji,sj->si", matrix, vector, precision=precise)


def compose(former, latter):
    return (product(latter[0], former[0]), applied(latter[0], former[1]) + latter[1])


def identity_map(members, tile_width):
    eye_block = jnp.broadcast_to(
        jnp.eye(tile_width, dtype=jnp.float32), (members, tile_width, tile_width)
    )
    return (eye_block, jnp.zeros((members, tile_width), jnp.float32))


def entry_maps(local_map, neutral):
    return entering(local_map, "reach", compose, neutral, False)


def exit_maps(local_map, neutral):
    return entering(local_map, "reach", compose, neutral, True)


def shards(
    reach_residual,
    chain_inv,
    chain_link,
    outlet_link,
    junction_inv,
    junction_residual,
    upper_junction,
    lower_junction,
    cell_cotangent,
    junction_cotangent,
):
    members, blocks, tile_width = reach_residual.shape
    owned_rows = junction_inv.shape[0]
    junctions = owned_rows * lax.axis_size("basin")
    final_reach = lax.axis_size("reach") - 1
    multiplier = jnp.einsum("skij,skjl->skil", chain_inv, chain_link, precision=precise)
    forced = jnp.einsum("skij,skj->ski", chain_inv, reach_residual, precision=precise)
    local_matrix = multiplier[:, 0]
    local_vector = forced[:, 0]
    for number in range(1, blocks):
        local_matrix = product(multiplier[:, number], local_matrix)
        local_vector = applied(multiplier[:, number], local_vector) + forced[:, number]
    neutral = identity_map(members, tile_width)
    entry_map = entry_maps((local_matrix, local_vector), neutral)
    outlet = compose(entry_map, (local_matrix, local_vector))
    schur_tile = product(outlet_link, outlet[0])
    outlet_push = applied(outlet_link, outlet[1])
    schur_tile, outlet_push = (
        from_root(schur_tile, "reach", final_reach),
        from_root(outlet_push, "reach", final_reach),
    )
    backward = cell_cotangent[:, blocks - 1]
    for number in range(blocks - 2, -1, -1):
        backward = cell_cotangent[:, number] + applied_transposed(
            multiplier[:, number + 1], backward
        )
    local_back = applied_transposed(multiplier[:, 0], backward)
    reverse_local = (jnp.swapaxes(local_matrix, 1, 2), local_back)
    leaving = exit_maps(reverse_local, neutral)
    head_value = applied(reverse_local[0], leaving[1]) + local_back
    upward = from_root(head_value, "reach", 0)
    junction_rows = jnp.arange(junctions, dtype=jnp.int32)[:, None]
    lower_onehot = (junction_rows == lower_junction[None, :]).astype(jnp.float32)
    upper_onehot = (junction_rows == upper_junction[None, :]).astype(jnp.float32)

    def section_terms(section_all):
        return outlet_push + applied(schur_tile, section_all[upper_junction])

    def adjoint_terms(relief_all):
        return upward + applied_transposed(schur_tile, relief_all[lower_junction])

    sections = jnp.zeros((owned_rows, tile_width), jnp.float32)
    adjoint = jnp.zeros((owned_rows, tile_width), jnp.float32)

    def gather_sections(values):
        return lax.all_gather(values, "basin", axis=0, tiled=True)

    def gather_relief(values):
        return lax.all_gather(values, "basin", axis=0, tiled=True)

    for sweep_index in range(SWEEPS):
        inflow_terms = outlet_push if sweep_index == 0 else section_terms(gather_sections(sections))
        placed = jnp.dot(lower_onehot, inflow_terms, precision=precise)
        inflow = lax.psum_scatter(placed, "basin", scatter_dimension=0, tiled=True)
        sections = applied(junction_inv, junction_residual + inflow)
    for sweep_index in range(SWEEPS):
        return_terms = (
            upward
            if sweep_index == 0
            else adjoint_terms(gather_relief(applied_transposed(junction_inv, adjoint)))
        )
        placed = jnp.dot(upper_onehot, return_terms, precision=precise)
        adjoint = junction_cotangent + lax.psum_scatter(
            placed, "basin", scatter_dimension=0, tiled=True
        )
    section_all = gather_sections(sections)
    relief_all = gather_relief(applied_transposed(junction_inv, adjoint))
    head_sections = section_all[upper_junction]
    tail_relief = relief_all[lower_junction]
    carried = applied(entry_map[0], head_sections) + entry_map[1]
    cell_rows = []
    for number in range(blocks):
        carried = applied(multiplier[:, number], carried) + forced[:, number]
        cell_rows.append(carried)
    cell_update = jnp.stack(cell_rows, axis=1)
    incoming = applied_transposed(outlet_link, tail_relief)
    carried = cell_cotangent[:, blocks - 1] + applied(leaving[0], incoming) + leaving[1]
    collected = [carried]
    for number in range(blocks - 2, -1, -1):
        carried = cell_cotangent[:, number] + applied_transposed(multiplier[:, number + 1], carried)
        collected.append(carried)
    cell_adjoint = jnp.stack(collected[::-1], axis=1)
    return (cell_update, sections, cell_adjoint, adjoint)


def solution(mesh):
    placed = (
        P("basin", "reach", None),
        P("basin", "reach", None, None),
        P("basin", "reach", None, None),
        P("basin", None, None),
        P("basin", None, None),
        P("basin", None),
        P("basin"),
        P("basin"),
        P("basin", "reach", None),
        P("basin", None),
    )
    return jax.shard_map(
        shards,
        mesh=mesh,
        in_specs=placed,
        out_specs=(
            P("basin", "reach", None),
            P("basin", None),
            P("basin", "reach", None),
            P("basin", None),
        ),
        check_vma=False,
    )
```

profile of v0, /device:TPU:8, one launch (start us, length us, event | category | flops | bytes accessed | tf_op | source)
XLA Modules:
  0.0 1940.1 jit_solution(3543780025443325133)
XLA Ops:
  8.4 2.5 fusion.138
  15.3 16.4 all-gather.9
  35.1 13.7 all-gather.4
  52.1 32.2 %while.35 = (s32[]{:T(128)}, f32[6,128,128]{2,1,0:T(8,128)S(1)}, f32[6,128]{1,0:T(8,128)S(1)}, s32[]{:T(128)}, f32[8,6,128,128]{3,2,1,0:T(8,128)}, /*index=5*/f3...) while((s32[]{:T(128)}, f32[6,128,128]{2,1,0:T(8,128)S(1)}, ...), condition=%wide.region_9.10_spmd.clone, body=%wide.region_8.9_spmd.clone.sunk | while | flops 152275968 | bytes 2777269 | solution.py:23
  85.3 4.5 all-gather.17.cloned.1.call-done
  90.7 32.1 %while.34 = (s32[]{:T(128)}, f32[6,128,128]{2,1,0:T(8,128)S(1)}, f32[6,128]{1,0:T(8,128)S(1)}, s32[]{:T(128)}, f32[8,6,128,128]{3,2,1,0:T(8,128)}, /*index=5*/f32[8,6,128]{2,1,0:T(8,128)}, s32[]{:T(128)}, s32[]{:T(128)}) while((s32[]{:T(128)}, f32[6,128,128]{2,1,0:T(8,128)S(1)}, f32[6,128]{1,0:T(8,128)S(1)}, s32[]{:T(128)}, ...), condition=%wide.region_1.2_spmd.clone, body=%wide.region_0.1_spmd.clone.sunk | while | flops 152275968 | bytes 2778223 | solution.py:23
  126.6 12.1 all-reduce.12
  144.1 2.7 fusion.18
  146.8 261.6 %all-reduce.27.cloned.1.call-done = (f32[384,128]{1,0:T(8,128)}, f32[384,128]{1,0:T(8,128)}) async-done(((f32[384,128]{1,0:T(8,128)}, f32[384,128]{1,0:T(8,128)}), (f32[384,128]{1,0:T(8,128)}, f32[384,128]{1,0:T(8,128)})) %all-reduce.27.cloned.1.call-update) | async-done | bytes 393232
  410.2 85.1 %all-gather.10 = f32[64,6,128]{2,1,0:T(8,128)} all-gather(f32[1,6,128]{2,1,0:T(8,128)S(1)} %bitcast.365), channel_id=1, replica_groups=mesh['basin'=64,'reach'=8] {'basin'}, dimensions={0}, use_global_device_ids=true | all-gather | bytes 199680 | tf_op jit(solution)/shard_map/all_gather | solution.py:121
  503.9 86.5 %all-gather.5 = f32[64,6,128]{2,1,0:T(8,128)} all-gather(f32[1,6,128]{2,1,0:T(8,128)S(1)} %bitcast.366), channel_id=1, replica_groups=mesh['basin'=64,'reach'=8] {'basin'}, dimensions={0}, use_global_device_ids=true | all-gather | bytes 199680 | tf_op jit(solution)/shard_map/all_gather | solution.py:118
  592.1 2.2 gather_fusion
  597.4 259.3 %all-reduce.25.cloned.1.call-done = (f32[384,128]{1,0:T(8,128)}, f32[384,128]{1,0:T(8,128)}) async-done(((f32[384,128]{1,0:T(8,128)}, f32[384,128]{1,0:T(8,128)}), (f32[384,128]{1,0:T(8,128)}, f32[384,128]{1,0:T(8,128)})) %all-reduce.25.cloned.1.call-update) | async-done | bytes 393232
  857.8 85.1 %all-gather.11 = f32[64,6,128]{2,1,0:T(8,128)} all-gather(f32[1,6,128]{2,1,0:T(8,128)S(1)} %bitcast.367), channel_id=1, replica_groups=mesh['basin'=64,'reach'=8] {'basin'}, dimensions={0}, use_global_device_ids=true | all-gather | bytes 199680 | tf_op jit(solution)/shard_map/all_gather | solution.py:121
  951.5 86.5 %all-gather.6 = f32[64,6,128]{2,1,0:T(8,128)} all-gather(f32[1,6,128]{2,1,0:T(8,128)S(1)} %bitcast.368), channel_id=1, replica_groups=mesh['basin'=64,'reach'=8] {'basin'}, dimensions={0}, use_global_device_ids=true | all-gather | bytes 199680 | tf_op jit(solution)/shard_map/all_gather | solution.py:118
  1039.6 2.2 gather_fusion.1
  1044.9 259.3 %all-reduce.23.cloned.1.call-done = (f32[384,128]{1,0:T(8,128)}, f32[384,128]{1,0:T(8,128)}) async-done(((f32[384,128]{1,0:T(8,128)}, f32[384,128]{1,0:T(8,128)}), (f32[384,128]{1,0:T(8,128)}, f32[384,128]{1,0:T(8,128)})) %all-reduce.23.cloned.1.call-update) | async-done | bytes 393232
  1305.4 85.1 %all-gather.12 = f32[64,6,128]{2,1,0:T(8,128)} all-gather(f32[1,6,128]{2,1,0:T(8,128)S(1)} %bitcast.369), channel_id=1, replica_groups=mesh['basin'=64,'reach'=8] {'basin'}, dimensions={0}, use_global_device_ids=true | all-gather | bytes 199680 | tf_op jit(solution)/shard_map/all_gather | solution.py:121
  1392.2 2.2 gather_fusion.6
  1399.2 86.7 %all-gather.7 = f32[64,6,128]{2,1,0:T(8,128)} all-gather(f32[1,6,128]{2,1,0:T(8,128)S(1)} %bitcast.370), channel_id=1, replica_groups=mesh['basin'=64,'reach'=8] {'basin'}, dimensions={0}, use_global_device_ids=true | all-gather | bytes 199680 | tf_op jit(solution)/shard_map/all_gather | solution.py:118
  1487.5 2.2 gather_fusion.2
  1492.8 259.4 %all-reduce.21.cloned.1.call-done = (f32[384,128]{1,0:T(8,128)}, f32[384,128]{1,0:T(8,128)}) async-done(((f32[384,128]{1,0:T(8,128)}, f32[384,128]{1,0:T(8,128)}), (f32[384,128]{1,0:T(8,128)}, f32[384,128]{1,0:T(8,128)})) %all-reduce.21.cloned.1.call-update) | async-done | bytes 393232
  1753.9 85.1 %all-gather.13 = f32[64,6,128]{2,1,0:T(8,128)} all-gather(f32[1,6,128]{2,1,0:T(8,128)S(1)} %bitcast.371), channel_id=1, replica_groups=mesh['basin'=64,'reach'=8] {'basin'}, dimensions={0}, use_global_device_ids=true | all-gather | bytes 199680 | tf_op jit(solution)/shard_map/all_gather | solution.py:121
  1848.0 81.0 %all-gather.8 = f32[64,6,128]{2,1,0:T(8,128)S(1)} all-gather(f32[1,6,128]{2,1,0:T(8,128)S(1)} %bitcast.363), channel_id=1, replica_groups=mesh['basin'=64,'reach'=8] {'basin'}, dimensions={0}, use_global_device_ids=true | all-gather | bytes 199680 | tf_op jit(solution)/shard_map/all_gather | solution.py:118
  (248 shorter events, 143.0 us)
Async XLA Ops:
  7.2 44.8 %all-gather.19.cloned.1.call-start = ((), (), s32[]{:S(2)}) async-start(), calls=%async_computation.2 | async-start | bytes 3538944 | tf_op jit(solution)/shard_map/all_gather | solution.py:12
  13.0 18.8 copy-start.22
  13.0 76.8 %all-gather.17.cloned.1.call-start = ((), (), s32[]{:S(2)}) async-start(), calls=%async_computation.1 | async-start | bytes 3538944 | tf_op jit(solution)/shard_map/all_gather | solution.py:12
  13.7 394.7 %all-reduce.27.cloned.1.call-start = ((), (), s32[]{:S(2)}) async-start(), calls=%async_computation.6 | async-start | bytes 786432
  13.8 38.2 %copy-start.4 = (f32[128,128]{1,0:T(8,128)}, f32[128,128]{1,0:T(8,128)S(1)}, u32[]{:S(2)}) copy-start(f32[128,128]{1,0:T(8,128)S(1)} %fusion.47) | copy-start | bytes 196612
  13.9 17.8 copy-start.12
  13.9 17.8 copy-start.14
  13.9 17.8 copy-start.16
  14.8 34.0 %copy-start.21 = (s32[6]{0:T(128)S(1)}, s32[6]{0:T(128)}, u32[]{:S(2)}) copy-start(s32[6]{0:T(128)} %param.21) | copy-start | bytes 76
  14.8 34.6 %copy-start.20 = (s32[6]{0:T(128)S(1)}, s32[6]{0:T(128)}, u32[]{:S(2)}) copy-start(s32[6]{0:T(128)} %param.20) | copy-start | bytes 76
  33.7 18.4 copy-start.5
  35.1 17.0 copy-start.11
  52.1 32.2 %copy-start.3 = (f32[6,128,128]{2,1,0:T(8,128)S(1)}, f32[6,128,128]{2,1,0:T(8,128)}, u32[]{:S(2)}) copy-start(f32[6,128,128]{2,1,0:T(8,128)} %copy-done.2) | copy-start | bytes 1179652
  138.7 3.4 copy-start.9
  141.9 357.2 %all-reduce.19.cloned.1.call-start = ((), (), s32[]{:S(2)}) async-start(), calls=%async_computation | async-start | bytes 786432 | tf_op jit(solution)/shard_map/psum | solution.py:28
  142.2 266.2 %copy-start.7 = (f32[6,128]{1,0:T(8,128)S(1)}, f32[6,128]{1,0:T(8,128)}, u32[]{:S(2)}) copy-start(f32[6,128]{1,0:T(8,128)} %param.23) | copy-start | bytes 9220
  142.2 266.2 %copy-start.8 = (f32[6,128]{1,0:T(8,128)S(1)}, f32[6,128]{1,0:T(8,128)}, u32[]{:S(2)}) copy-start(f32[6,128]{1,0:T(8,128)} %param.19) | copy-start | bytes 9220
  142.2 267.5 %copy-start.1 = (f32[6,128,128]{2,1,0:T(8,128)S(1)}, f32[6,128,128]{2,1,0:T(8,128)}, u32[]{:S(2)}) copy-start(f32[6,128,128]{2,1,0:T(8,128)} %param.18) | copy-start | bytes 1179652
  146.8 709.9 %all-reduce.25.cloned.1.call-start = ((), (), s32[]{:S(2)}) async-start(), calls=%async_computation.5 | async-start | bytes 786432
  597.3 707.0 %all-reduce.23.cloned.1.call-start = ((), (), s32[]{:S(2)}) async-start(), calls=%async_computation.4 | async-start | bytes 786432
  1044.9 707.3 %all-reduce.21.cloned.1.call-start = ((), (), s32[]{:S(2)}) async-start(), calls=%async_computation.3 | async-start | bytes 786432
  1752.9 92.1 %copy-start.13 = (f32[6,1,128]{2,1,0:T(1,128)S(1)}, f32[6,1,128]{2,1,0:T(1,128)}, u32[]{:S(2)}) copy-start(f32[6,1,128]{2,1,0:T(1,128)} %copy-done.12) | copy-start | bytes 9220
  1845.5 85.7 %copy-start.6 = (f32[6,3,1,128]{3,0,1,2:T(8,128)S(1)}, f32[6,3,1,128]{3,0,1,2:T(8,128)}, u32[]{:S(2)}) copy-start(f32[6,3,1,128]{3,0,1,2:T(8,128)} %copy-done.5) | copy-start | bytes 27652
  1848.0 84.6 %copy-start.18 = (f32[6,1,128]{2,0,1:T(8,128)}, f32[6,1,128]{2,0,1:T(8,128)S(1)}, u32[]{:S(2)}) copy-start(f32[6,1,128]{2,0,1:T(8,128)S(1)} %copy.279) | copy-start | bytes 9220
  (7 other events, 14.3 us)
Sparse Core Ops, SparseCore 0:
  13.1 38.8 all-gather.18
  54.1 35.6 all-gather.16
  142.1 266.3 all-reduce.26
  410.6 68.1 all-reduce.18
  597.5 259.1 all-reduce.24
  1045.0 259.2 all-reduce.22
  1492.9 259.2 all-reduce.20
where the time goes:
time: 1940 us
  waiting for transfers between devices  1040 us (54%)
  blocking collectives  723 us (37%)
  matrix products  102 us (5%)
  local copies, waits for them, and re-layouts  34.4 us (2%)
  other arithmetic  19.5 us (1%)
    unnamed x11, waiting for transfers between devices  1040 us
    all_gather x4, blocking collectives, gather_sections(): return lax.all_gather(values, 'basin', axis=0, tiled=True)  341 us
    all_gather x4, blocking collectives, gather_relief(): return lax.all_gather(values, 'basin', axis=0, tiled=True)  340 us
    dot_general x33, matrix products, applied(): return jnp.einsum('sij,sj->si', matrix, vector, precision=precise)  43.8 us
  transfers between devices with their start and end apart: 7, of which 5 were waited for; matrix products, arithmetic and copies ran while one was open for 3% of the time, Pallas kernels for 0%

commit v1 on v0

--- a/solution.py
+++ b/solution.py
@@ -1,10 +1,22 @@
+import functools
 import jax
 import jax.numpy as jnp
 from jax import lax
 from jax.sharding import PartitionSpec as P
+from jax.lax import all_to_all, axis_size
 
 SWEEPS = 4
 precise = lax.Precision.HIGHEST
+
+
+def lift_cubes(field, which_axis):
+    formed = tuple((field for _ in range(axis_size(which_axis))))
+    newest = jnp.stack(formed, axis=0)
+    earlier = all_to_all(newest, split_axis=0, concat_axis=0, axis_name=which_axis)
+    return jnp.concatenate(earlier, axis=0)
+
+
+divide_shifts_all = functools.partial(lift_cubes, which_axis="basin")
 
 
 def entering(x, axis, combine, identity, reverse):
@@ -118,7 +130,7 @@
         return lax.all_gather(values, "basin", axis=0, tiled=True)
 
     def gather_relief(values):
-        return lax.all_gather(values, "basin", axis=0, tiled=True)
+        return divide_shifts_all(values)
 
     for sweep_index in range(SWEEPS):
         inflow_terms = outlet_push if sweep_index == 0 else section_terms(gather_sections(sections))

time: 1940 us -> 1660 us (0.86)
  blocking collectives: 723 us -> 393 us
  starting transfers between devices: 0.47 us -> 35.7 us
    all_gather x4 -> x0, blocking collectives: 340 us -> none  [gather_relief(): return lax.all_gather(values, 'basin', axis=0, tiled=True)]
    all_to_all x0 -> x4, starting transfers between devices: none -> 35.4 us  [lift_cubes(): all_to_all(newest, split_axis=0, concat_axis=0, axis_name=which_axis)]
  transfers between devices with their start and end apart: 7 -> 11, of which waited for: 5 -> 6; matrix products, arithmetic and copies ran while one was open for 3% -> 5% of each run, Pallas kernels for 0% -> 0%
where the time goes in v1:
time: 1660 us
  waiting for transfers between devices  1050 us (63%)
  blocking collectives  393 us (24%)
  matrix products  102 us (6%)
  local copies, waits for them, and re-layouts  36.6 us (2%)
  starting transfers between devices  35.7 us (2%)
  other arithmetic  23.9 us (1%)
    unnamed x11, waiting for transfers between devices  1050 us
    all_gather x4, blocking collectives, gather_sections(): return lax.all_gather(values, 'basin', axis=0, tiled=True)  349 us
    dot_general x33, matrix products, applied(): return jnp.einsum('sij,sj->si', matrix, vector, precision=precise)  43.8 us
    all_to_all x4, starting transfers between devices, lift_cubes(): all_to_all(newest, split_axis=0, concat_axis=0, axis_name=which_axis)  35.4 us
  transfers between devices with their start and end apart: 11, of which 6 were waited for; matrix products, arithmetic and copies ran while one was open for 5% of the time, Pallas kernels for 0%

profile of v1, /device:TPU:8, one launch (start us, length us, event | category | flops | bytes accessed | tf_op | source)
XLA Modules:
  0.0 1659.0 jit_solution(13767590875661819132)
XLA Ops:
  8.4 2.5 fusion.138
  15.3 16.3 all-gather.9
  35.0 13.9 all-gather.4
  52.1 32.2 %while.35 = (s32[]{:T(128)}, f32[6,128,128]{2,1,0:T(8,128)S(1)}, f32[6,128]{1,0:T(8,128)S(1)}, s32[]{:T(128)}, f32[8,6,128,128]{3,2,1,0:T(8,128)}, /*index=5*/f3...) while((s32[]{:T(128)}, f32[6,128,128]{2,1,0:T(8,128)S(1)}, ...), condition=%wide.region_9.10_spmd.clone, body=%wide.region_8.9_spmd.clone.sunk | while | flops 152275968 | bytes 2777269 | solution.py:35
  85.3 4.4 all-gather.13.cloned.1.call-done
  90.6 32.1 %while.34 = (s32[]{:T(128)}, f32[6,128,128]{2,1,0:T(8,128)S(1)}, f32[6,128]{1,0:T(8,128)S(1)}, s32[]{:T(128)}, f32[8,6,128,128]{3,2,1,0:T(8,128)}, /*index=5*/f32[8,6,128]{2,1,0:T(8,128)}, s32[]{:T(128)}, s32[]{:T(128)}) while((s32[]{:T(128)}, f32[6,128,128]{2,1,0:T(8,128)S(1)}, f32[6,128]{1,0:T(8,128)S(1)}, s32[]{:T(128)}, ...), condition=%wide.region_1.2_spmd.clone, body=%wide.region_0.1_spmd.clone.sunk | while | flops 152275968 | bytes 2778223 | solution.py:35
  127.8 13.0 all-reduce.12
  148.5 2.5 fusion.139
  151.0 259.7 %all-reduce.27.cloned.1.call-done = (f32[384,128]{1,0:T(8,128)}, f32[384,128]{1,0:T(8,128)}) async-done(((f32[384,128]{1,0:T(8,128)}, f32[384,128]{1,0:T(8,128)}), (f32[384,128]{1,0:T(8,128)}, f32[384,128]{1,0:T(8,128)})) %all-reduce.27.cloned.1.call-update) | async-done | bytes 393232
  413.2 8.9 all-to-all-start
  422.1 2.8 fusion.18
  426.4 88.7 %all-gather.5 = f32[64,6,128]{2,1,0:T(8,128)} all-gather(f32[1,6,128]{2,1,0:T(8,128)S(1)} %bitcast.362), channel_id=1, replica_groups=mesh['basin'=64,'reach'=8] {'basin'}, dimensions={0}, use_global_device_ids=true | all-gather | bytes 199680 | tf_op jit(solution)/shard_map/all_gather | solution.py:130
  516.7 2.2 gather_fusion
  523.6 2.2 gather_fusion.4
  529.2 262.0 %all-reduce.25.cloned.1.call-done = (f32[384,128]{1,0:T(8,128)}, f32[384,128]{1,0:T(8,128)}) async-done(((f32[384,128]{1,0:T(8,128)}, f32[384,128]{1,0:T(8,128)}), (f32[384,128]{1,0:T(8,128)}, f32[384,128]{1,0:T(8,128)})) %all-reduce.25.cloned.1.call-update) | async-done | bytes 393232
  793.0 8.9 all-to-all-start.1
  803.4 88.7 %all-gather.6 = f32[64,6,128]{2,1,0:T(8,128)} all-gather(f32[1,6,128]{2,1,0:T(8,128)S(1)} %bitcast.364), channel_id=1, replica_groups=mesh['basin'=64,'reach'=8] {'basin'}, dimensions={0}, use_global_device_ids=true | all-gather | bytes 199680 | tf_op jit(solution)/shard_map/all_gather | solution.py:130
  893.7 2.2 gather_fusion.1
  906.1 262.0 %all-reduce.23.cloned.1.call-done = (f32[384,128]{1,0:T(8,128)}, f32[384,128]{1,0:T(8,128)}) async-done(((f32[384,128]{1,0:T(8,128)}, f32[384,128]{1,0:T(8,128)}), (f32[384,128]{1,0:T(8,128)}, f32[384,128]{1,0:T(8,128)})) %all-reduce.23.cloned.1.call-update) | async-done | bytes 393232
  1170.0 8.9 all-to-all-start.2
  1180.3 88.9 %all-gather.7 = f32[64,6,128]{2,1,0:T(8,128)} all-gather(f32[1,6,128]{2,1,0:T(8,128)S(1)} %bitcast.366), channel_id=1, replica_groups=mesh['basin'=64,'reach'=8] {'basin'}, dimensions={0}, use_global_device_ids=true | all-gather | bytes 199680 | tf_op jit(solution)/shard_map/all_gather | solution.py:130
  1283.3 262.0 %all-reduce.21.cloned.1.call-done = (f32[384,128]{1,0:T(8,128)}, f32[384,128]{1,0:T(8,128)}) async-done(((f32[384,128]{1,0:T(8,128)}, f32[384,128]{1,0:T(8,128)}), (f32[384,128]{1,0:T(8,128)}, f32[384,128]{1,0:T(8,128)})) %all-reduce.21.cloned.1.call-update) | async-done | bytes 393232
  1547.8 8.9 all-to-all-start.3
  1558.1 83.0 %all-gather.8 = f32[64,6,128]{2,1,0:T(8,128)S(1)} all-gather(f32[1,6,128]{2,1,0:T(8,128)S(1)} %bitcast.359), channel_id=1, replica_groups=mesh['basin'=64,'reach'=8] {'basin'}, dimensions={0}, use_global_device_ids=true | all-gather | bytes 199680 | tf_op jit(solution)/shard_map/all_gather | solution.py:130
  (254 shorter events, 150.6 us)
Async XLA Ops:
  7.2 44.8 %all-gather.15.cloned.1.call-start = ((), (), s32[]{:S(2)}) async-start(), calls=%async_computation.6 | async-start | bytes 3538944 | tf_op jit(solution)/shard_map/all_gather | solution.py:24
  13.0 18.7 %copy-start.21 = (f32[6,3,128]{2,1,0:T(4,128)S(1)}, f32[6,3,128]{2,1,0:T(4,128)}, u32[]{:S(2)}) copy-start(f32[6,3,128]{2,1,0:T(4,128)} %param.14) | copy-start | bytes 27652
  13.0 76.7 %all-gather.13.cloned.1.call-start = ((), (), s32[]{:S(2)}) async-start(), calls=%async_computation.5 | async-start | bytes 3538944 | tf_op jit(solution)/shard_map/all_gather | solution.py:24
  13.7 396.9 %all-reduce.27.cloned.1.call-start = ((), (), s32[]{:S(2)}) async-start(), calls=%async_computation.10 | async-start | bytes 786432
  13.8 38.2 %copy-start.5 = (f32[128,128]{1,0:T(8,128)}, f32[128,128]{1,0:T(8,128)S(1)}, u32[]{:S(2)}) copy-start(f32[128,128]{1,0:T(8,128)S(1)} %fusion.47) | copy-start | bytes 196612
  13.9 17.8 %copy-start.11 = (f32[6,1,128]{2,1,0:T(1,128)}, f32[6,1,128]{2,1,0:T(1,128)S(1)}, u32[]{:S(2)}) copy-start(f32[6,1,128]{2,1,0:T(1,128)S(1)} %get-tuple-element.373) | copy-start | bytes 9220
  13.9 17.7 %copy-start.13 = (f32[6,1,128]{2,1,0:T(1,128)}, f32[6,1,128]{2,1,0:T(1,128)S(1)}, u32[]{:S(2)}) copy-start(f32[6,1,128]{2,1,0:T(1,128)S(1)} %get-tuple-element.374) | copy-start | bytes 9220
  13.9 17.7 %copy-start.15 = (f32[6,1,128]{2,1,0:T(1,128)}, f32[6,1,128]{2,1,0:T(1,128)S(1)}, u32[]{:S(2)}) copy-start(f32[6,1,128]{2,1,0:T(1,128)S(1)} %get-tuple-element.375) | copy-start | bytes 9220
  14.8 34.2 %copy-start.19 = (s32[6]{0:T(128)S(1)}, s32[6]{0:T(128)}, u32[]{:S(2)}) copy-start(s32[6]{0:T(128)} %param.21) | copy-start | bytes 76
  14.8 34.7 %copy-start.20 = (s32[6]{0:T(128)S(1)}, s32[6]{0:T(128)}, u32[]{:S(2)}) copy-start(s32[6]{0:T(128)} %param.20) | copy-start | bytes 76
  33.6 18.5 %copy-start.6 = (f32[6,3,1,128]{3,0,1,2:T(8,128)}, f32[6,3,1,128]{3,0,1,2:T(8,128)S(1)}, u32[]{:S(2)}) copy-start(f32[6,3,1,128]{3,0,1,2:T(8,128)S(1)} %copy.276) | copy-start | bytes 27652
  52.0 32.2 %copy-start.3 = (f32[6,128,128]{2,1,0:T(8,128)S(1)}, f32[6,128,128]{2,1,0:T(8,128)}, u32[]{:S(2)}) copy-start(f32[6,128,128]{2,1,0:T(8,128)} %copy-done.2) | copy-start | bytes 1179652
  125.4 285.3 %copy-start.8 = (f32[6,128]{1,0:T(8,128)S(1)}, f32[6,128]{1,0:T(8,128)}, u32[]{:S(2)}) copy-start(f32[6,128]{1,0:T(8,128)} %param.23) | copy-start | bytes 9220
  125.4 285.3 %copy-start.9 = (f32[6,128]{1,0:T(8,128)S(1)}, f32[6,128]{1,0:T(8,128)}, u32[]{:S(2)}) copy-start(f32[6,128]{1,0:T(8,128)} %param.19) | copy-start | bytes 9220
  125.4 286.6 %copy-start.1 = (f32[6,128,128]{2,1,0:T(8,128)S(1)}, f32[6,128,128]{2,1,0:T(8,128)}, u32[]{:S(2)}) copy-start(f32[6,128,128]{2,1,0:T(8,128)} %param.18) | copy-start | bytes 1179652
  413.2 108.8 %all-to-all-start = ((f32[64,6,128]{2,1,0:T(8,128)}), f32[64,6,128]{2,1,0:T(8,128)}, u32[]{:S(2)}, u32[]{:S(2)}) async-start(f32[64,6,128]{2,1,0:T(8,128)} %stack.28), calls=%async_computation | async-start | bytes 524288 | tf_op jit(solution)/shard_map/all_to_all | solution.py:15
  422.0 96.9 %all-reduce.19.cloned.1.call-start = ((), (), s32[]{:S(2)}) async-start(), calls=%async_computation.4 | async-start | bytes 786432 | tf_op jit(solution)/shard_map/psum | solution.py:40
  424.9 366.3 %all-reduce.25.cloned.1.call-start = ((), (), s32[]{:S(2)}) async-start(), calls=%async_computation.9 | async-start | bytes 786432
  793.0 105.9 %all-to-all-start.1 = ((f32[64,6,128]{2,1,0:T(8,128)}), f32[64,6,128]{2,1,0:T(8,128)}, u32[]{:S(2)}, u32[]{:S(2)}) async-start(f32[64,6,128]{2,1,0:T(8,128)} %stack.29), calls=%async_computation.1 | async-start | bytes 524288 | tf_op jit(solution)/shard_map/all_to_all | solution.py:15
  801.9 366.2 %all-reduce.23.cloned.1.call-start = ((), (), s32[]{:S(2)}) async-start(), calls=%async_computation.8 | async-start | bytes 786432
  1170.0 106.1 %all-to-all-start.2 = ((f32[64,6,128]{2,1,0:T(8,128)}), f32[64,6,128]{2,1,0:T(8,128)}, u32[]{:S(2)}, u32[]{:S(2)}) async-start(f32[64,6,128]{2,1,0:T(8,128)} %stack.30), calls=%async_computation.2 | async-start | bytes 524288 | tf_op jit(solution)/shard_map/all_to_all | solution.py:15
  1178.8 366.5 %all-reduce.21.cloned.1.call-start = ((), (), s32[]{:S(2)}) async-start(), calls=%async_computation.7 | async-start | bytes 786432
  1547.8 100.0 %all-to-all-start.3 = ((f32[64,6,128]{2,1,0:T(8,128)}), f32[64,6,128]{2,1,0:T(8,128)}, u32[]{:S(2)}, u32[]{:S(2)}) async-start(f32[64,6,128]{2,1,0:T(8,128)} %stack.31), calls=%async_computation.3 | async-start | bytes 524288 | tf_op jit(solution)/shard_map/all_to_all | solution.py:15
  1558.1 89.0 %copy-start.17 = (f32[6,1,128]{2,0,1:T(8,128)}, f32[6,1,128]{2,0,1:T(8,128)S(1)}, u32[]{:S(2)}) copy-start(f32[6,1,128]{2,0,1:T(8,128)S(1)} %copy.279) | copy-start | bytes 9220
  (10 other events, 47.4 us)
Sparse Core Ops, SparseCore 0:
  13.1 38.8 all-gather.14
  54.1 35.5 all-gather.12
  144.2 266.4 all-reduce.26
  425.0 74.3 all-reduce.18
  529.3 261.8 all-reduce.24
  906.2 261.8 all-reduce.22
  1283.4 261.8 all-reduce.20
